TPU v7x, 256 devices: a whole 4x4x8 slice. The times are simulated.
256 devices in a mesh: section: 8 (over y, x_lo), lat: 32 (over x_hi, z, core).
Axes of the slice: x: 4 (x_hi: 2, x_lo: 2; x = x_hi * 2 + x_lo), y: 4, z: 8, core: 2. Of those that a mesh axis runs over, the one named last changes fastest.
Arguments:
- stacked: bfloat16 [1024, 16384], P('lat', 'section'), may hold values from -6 to 6
- enc_weight: bfloat16 [16384, 16384], P('section', 'lat'), may hold values from -0.046875 to 0.046875
- enc_bias: float32 [16384], P('lat'), may hold values from -3 to 3
- dec_weight: bfloat16 [16384, 16384], P('lat', 'section'), may hold values from -0.046875 to 0.046875
- dec_bias: float32 [16384], P('section'), may hold values from -3 to 3
- active: int32 [1024, 16384], P(None, 'lat'), may hold values 0 or 1
- upstream: bfloat16 [1024, 16384], P('lat', 'section'), may hold values from -0.3984375 to 0.3984375
Outputs:
- rebuilt: bfloat16 [1024, 16384], P('lat', 'section')
- enc_grad: bfloat16 [16384, 16384], P('section', 'lat')
- dec_grad: bfloat16 [16384, 16384], P('lat', 'section')
All inputs are finite; a program needn't handle non-finite values. No bound on the sum of `active` on one device may be relied on, other than what follows from the above.
Results may differ from a plain program's by a relative error of at most 0.0049.
Values may be sent and summed in bfloat16 or wider, within the bound.
A program may use at most 128 MiB of HBM per device.

v0:
```python
import jax
import jax.numpy as jnp
from jax import lax
from jax.sharding import PartitionSpec as P


def per_device(stacked, enc_weight, enc_bias, dec_weight, dec_bias, active, upstream):
    gating = active.astype(jnp.float32)
    stacked_all = lax.all_gather(stacked, "lat", axis=0, tiled=True)
    partial_value = jnp.dot(stacked_all, enc_weight, preferred_element_type=jnp.float32)
    preact = lax.psum(partial_value, "section") + enc_bias
    latent = (gating * preact).astype(jnp.bfloat16)
    summed = lax.psum_scatter(
        jnp.dot(latent, dec_weight, preferred_element_type=jnp.float32),
        "lat",
        scatter_dimension=0,
        tiled=True,
    )
    rebuilt = (summed + dec_bias).astype(jnp.bfloat16)
    upstream_all = lax.all_gather(upstream, "lat", axis=0, tiled=True)
    dec_grad = lax.dot_general(
        latent, upstream_all, (((0,), (0,)), ((), ())), preferred_element_type=jnp.float32
    ).astype(jnp.bfloat16)
    grad_part = lax.dot_general(
        upstream_all, dec_weight, (((1,), (1,)), ((), ())), preferred_element_type=jnp.float32
    )
    latent_grad = lax.psum(grad_part, "section")
    pre_grad = (gating * latent_grad).astype(jnp.bfloat16)
    enc_grad = lax.dot_general(
        stacked_all, pre_grad, (((0,), (0,)), ((), ())), preferred_element_type=jnp.float32
    ).astype(jnp.bfloat16)
    return (rebuilt, enc_grad, dec_grad)


def solution(mesh):
    placed = (
        P("lat", "section"),
        P("section", "lat"),
        P("lat"),
        P("lat", "section"),
        P("section"),
        P(None, "lat"),
        P("lat", "section"),
    )
    return jax.shard_map(
        per_device,
        mesh=mesh,
        in_specs=placed,
        out_specs=(P("lat", "section"), P("section", "lat"), P("lat", "section")),
        check_vma=False,
    )
```

profile of v0, /device:TPU:8, one launch (start us, length us, event | category | flops | bytes accessed | tf_op | source)
XLA Modules:
  0.0 549.7 jit_solution(16592056367653962013)
XLA Ops:
  7.2 0.0 copy-start
  7.2 0.0 all-gather.5.cloned.1.call-start
  7.2 0.7 all-gather.5.cloned.1.call-update
  7.9 0.0 all-gather.3.cloned.1.call-start
  8.0 0.7 all-gather.3.cloned.1.call-update
  8.7 0.0 all-reduce.3.cloned.1.call-start
  8.7 91.8 %all-gather.5.cloned.1.call-done = bf16[1024,2048]{1,0:T(8,128)(2,1)} async-done(((bf16[32,2048]{1,0:T(8,128)(2,1)}), bf16[1024,2048]{1,0:T(8,128)(2,1)}) %all-gather.5.cloned.1.call-update) | async-done | bytes 4194320 | tf_op jit(solution)/shard_map/all_gather | solution.py:20
  100.5 0.0 copy-done
  100.5 5.9 %fusion.3 = f32[1024,512]{1,0:T(8,128)} fusion(bf16[1024,2048]{1,0:T(8,128)(2,1)} %all-gather.5.cloned.1.call-done, bf16[512,2048]{1,0:T(8,128)(2,1)S(1)} %copy-done), kind=kOutput, calls=%fused_computation.8 | convolution fusion | flops 2147483648 | bytes 8388608 | tf_op jit(solution)/shard_map/dot_general | solution.py:24
  106.4 80.4 %all-gather.3.cloned.1.call-done = bf16[1024,2048]{1,0:T(8,128)(2,1)} async-done(((bf16[32,2048]{1,0:T(8,128)(2,1)}), bf16[1024,2048]{1,0:T(8,128)(2,1)}) %all-gather.3.cloned.1.call-update) | async-done | bytes 4194320 | tf_op jit(solution)/shard_map/all_gather | solution.py:9
  186.8 6.5 %fusion.1 = f32[1024,512]{1,0:T(8,128)} fusion(bf16[1024,2048]{1,0:T(8,128)(2,1)} %all-gather.3.cloned.1.call-done, bf16[2048,512]{1,0:T(8,128)(2,1)} %param.8), kind=kOutput, calls=%fused_computation.6 | convolution fusion | flops 2147483648 | bytes 8388608 | tf_op jit(solution)/shard_map/dot_general | solution.py:10
  193.4 0.0 copy-start.2
  193.4 0.0 all-reduce.3.cloned.1.call-update
  193.4 0.0 reduce-scatter.2.cloned.1.call-start
  193.4 184.4 %all-reduce.3.cloned.1.call-done = (f32[1024,512]{1,0:T(8,128)}, f32[1024,512]{1,0:T(8,128)}) async-done(((f32[1024,512]{1,0:T(8,128)}, f32[1024,512]{1,0:T(8,128)}), (f32[1024,512]{1,0:T(8,128)}, f32[1024,512]{1,0:T(8,128)})) %all-reduce.3.cloned.1.call-update) | async-done | bytes 4194320 | tf_op jit(solution)/shard_map/psum | solution.py:11
  377.8 0.0 copy-done.2
  377.8 2.8 multiply_convert_fusion.1
  380.6 5.6 %fusion.2 = f32[1024,2048]{1,0:T(8,128)} fusion(bf16[1024,512]{1,0:T(8,128)(2,1)S(1)} %multiply_convert_fusion.1, bf16[512,2048]{1,0:T(8,128)(2,1)S(1)} %copy-done), kind=kOutput, calls=%fused_computation.7 | convolution fusion | flops 2147483648 | bytes 11534336 | tf_op jit(solution)/shard_map/dot_general | solution.py:14
  386.2 0.0 reduce-scatter.2.cloned.1.call-update
  386.2 7.3 %fusion = bf16[2048,512]{0,1:T(8,128)(2,1)} fusion(bf16[1024,2048]{1,0:T(8,128)(2,1)} %all-gather.3.cloned.1.call-done, f32[1024,512]{1,0:T(8,128)} %get-tuple-element.7, s32[1024,512]{1,0:T(8,128)} %param.12), kind=kOutput, calls=%fused_computation.2 | convolution fusion | flops 2150105088 | bytes 10485760 | tf_op jit(solution)/shard_map/dot_general | solution.py:29
  393.5 3.9 copy.10
  397.5 0.0 copy-start.1
  397.5 6.0 %convolution_convert_fusion = bf16[512,2048]{1,0:T(8,128)(2,1)} fusion(bf16[1024,512]{1,0:T(8,128)(2,1)S(1)} %multiply_convert_fusion.1, bf16[1024,2048]{1,0:T(8,128)(2,1)} %all-gather.5.cloned.1.call-done), kind=kOutput, calls=%fused_computation | convolution fusion | flops 2148532224 | bytes 7340032 | tf_op jit(solution)/shard_map/dot_general | solution.py:21
  403.5 138.0 %reduce-scatter.2.cloned.1.call-done = f32[32,2048]{1,0:T(8,128)} async-done(((f32[1024,2048]{1,0:T(8,128)}), f32[32,2048]{1,0:T(8,128)}) %reduce-scatter.2.cloned.1.call-update) | async-done | bytes 262160 | tf_op jit(solution)/shard_map/reduce_scatter | solution.py:13
  541.5 0.0 copy-done.1
  541.5 1.6 add_convert_fusion
Async XLA Ops:
  7.2 93.4 %copy-start = (bf16[512,2048]{1,0:T(8,128)(2,1)S(1)}, bf16[512,2048]{1,0:T(8,128)(2,1)}, u32[]{:S(2)}) copy-start(bf16[512,2048]{1,0:T(8,128)(2,1)} %param.10) | copy-start | bytes 6291460
  7.2 93.4 %all-gather.5.cloned.1.call-start = ((), (), s32[]{:S(2)}) async-start(), calls=%async_computation.3 | async-start | bytes 4325376 | tf_op jit(solution)/shard_map/all_gather | solution.py:20
  7.9 178.9 %all-gather.3.cloned.1.call-start = ((), (), s32[]{:S(2)}) async-start(), calls=%async_computation.1 | async-start | bytes 4325376 | tf_op jit(solution)/shard_map/all_gather | solution.py:9
  8.7 369.2 %all-reduce.3.cloned.1.call-start = ((), (), s32[]{:S(2)}) async-start(), calls=%async_computation.4 | async-start | bytes 8388608 | tf_op jit(solution)/shard_map/psum | solution.py:11
  193.4 184.5 %copy-start.2 = (f32[512]{0:T(512)S(1)}, f32[512]{0:T(512)}, u32[]{:S(2)}) copy-start(f32[512]{0:T(512)} %param.9) | copy-start | bytes 6148
  193.4 348.1 %reduce-scatter.2.cloned.1.call-start = ((), (), s32[]{:S(2)}) async-start(), calls=%async_computation.2 | async-start | bytes 8650752 | tf_op jit(solution)/shard_map/reduce_scatter | solution.py:13
  397.5 144.0 %copy-start.1 = (f32[2048]{0:T(1024)S(1)}, f32[2048]{0:T(1024)}, u32[]{:S(2)}) copy-start(f32[2048]{0:T(1024)} %param.11) | copy-start | bytes 24580
Sparse Core Ops, SparseCore 0:
  10.8 89.6 all-gather.4
  103.3 83.4 all-gather.2
  193.5 184.2 all-reduce.2
  386.3 155.1 reduce-scatter.1
where the time goes:
time: 550 us
  waiting for transfers between devices  496 us (90%)
  matrix products  31.3 us (6%)
  between operations  13.8 us (3%)
    psum x1, waiting for transfers between devices, per_device(): preact = lax.psum(partial_value, 'section') + enc_bias  184 us
    reduce_scatter x1, waiting for transfers between devices, per_device(): lax.psum_scatter(jnp.dot(latent, dec_weight, preferred_element_type=jnp.f...  138 us
    all_gather x1, waiting for transfers between devices, per_device(): upstream_all = lax.all_gather(upstream, 'lat', axis=0, tiled=True)  91.8 us
    all_gather x1, waiting for transfers between devices, per_device(): stacked_all = lax.all_gather(stacked, 'lat', axis=0, tiled=True)  80.4 us
  transfers between devices with their start and end apart: 4, of which 4 were waited for; matrix products, arithmetic and copies ran while one was open for 4% of the time, Pallas kernels for 0%

commit v1 on v0

v1 whole, which is shorter than its diff:
```python
import jax
import jax.numpy as jnp
from jax import lax
from jax.experimental import pallas as pl
from jax.experimental.pallas import tpu as pltpu
from jax.sharding import PartitionSpec as P

F32, BF16 = jnp.float32, jnp.bfloat16
MESH = pl.DeviceIdType.MESH
B = 32
FEAT = 2048
LATS = 512
TOK = 1024
CH = 256

PLACE = {1: 0, 7: 1, 2: 2, 6: 3, 3: 4, 5: 5, 0: 6, 4: 7}
PAIRS = ((1, 7), (2, 6), (3, 5), (0, 4))


def row(d, core, half):
    return PLACE[d] * 128 + core * 64 + half * 32


GZ = (
    (-1, 0, 0, 1), (1, 0, 0, 7), (-1, 1, 0, 2), (1, 7, 0, 6), (-1, 2, 0, 3), (1, 6, 0, 5),
    (-1, 3, 0, 4), (-1, 2, 1, 3), (1, 6, 1, 5), (1, 5, 1, 4),
)
GZ_INTO = {(there, half): i for i, (_, _, half, there) in enumerate(GZ)}
GX = (0, 1, 7, 2, 6)

RZ = (
    (1, 4, 0, 3), (-1, 4, 1, 5), (1, 3, 1, 2), (-1, 5, 0, 6), (1, 3, 0, 2), (-1, 5, 1, 6),
    (1, 2, 0, 1), (-1, 6, 0, 7), (1, 1, 0, 0), (-1, 7, 0, 0),
)
RZ_OF = {(here, half): i for i, (_, here, half, _) in enumerate(RZ)}


def rz_into(d, half):
    return [i for i, (_, _, h, there) in enumerate(RZ) if (there, h) == (d, half)]


def kernel(
    x_hbm, we_hbm, be_hbm, wd_hbm, bd_hbm, act_hbm, up_hbm,
    reb_hbm, ge_hbm, gd_hbm,
    xs, us, we, wd, be, bd, act,
    part, full, own, yin, xout, xin, lat, pre,
    dec, cin, stage, zin, xrin, ge, gd, reb,
    load_sem, store_sem, gz_s, gz_r, gx_s, gx_r, gc_s, gc_r,
    ry_s, ry_r, rx_s, rx_r, ax_s, ax_r, ay_s, ay_r,
    dc_s, dc_r, rz_s, rz_r, xr_s, xr_r,
):
    s = lax.axis_index("section")
    l = lax.axis_index("lat")
    y, xl = s // 2, lax.rem(s, 2)
    xh, z, c = l // 16, lax.rem(l, 16) // 2, lax.rem(l, 2)

    def at_lat(h, zz, cc):
        return h * 16 + zz * 2 + cc

    zdev = {
        1: (s, at_lat(xh, lax.rem(z + 1, 8), c)),
        -1: (s, at_lat(xh, lax.rem(z + 7, 8), c)),
    }
    xdev = (s, at_lat(1 - xh, z, c))
    cdev = (s, at_lat(xh, z, 1 - c))
    ypos = [lax.rem(y + k, 4) for k in (1, 2, 3)]
    ydev = [(p * 2 + xl, l) for p in ypos]
    sdev = (y * 2 + 1 - xl, l)

    def remote(src, dst, ssem, rsem, dev):
        return pltpu.make_async_remote_copy(
            src_ref=src, dst_ref=dst, send_sem=ssem, recv_sem=rsem, device_id=dev, device_id_type=MESH
        )

    mine = pl.ds(row(0, 0, 0), B)
    loads = [
        pltpu.make_async_copy(x_hbm, xs.at[mine], load_sem.at[0]),
        pltpu.make_async_copy(up_hbm, us.at[mine], load_sem.at[1]),
        pltpu.make_async_copy(we_hbm, we, load_sem.at[2]),
        pltpu.make_async_copy(wd_hbm, wd, load_sem.at[3]),
        pltpu.make_async_copy(be_hbm, be, load_sem.at[4]),
        pltpu.make_async_copy(bd_hbm, bd, load_sem.at[5]),
    ]
    pair, score, shalf = s // 4, lax.rem(s, 4) // 2, lax.rem(s, 2)
    for q, (d0, d1) in enumerate(PAIRS):
        dist = d0 + pair * (d1 - d0)
        owner = at_lat(
            lax.rem(xh + shalf, 2), lax.rem(z + dist, 8), lax.rem(c + score, 2)
        )
        loads.append(
            pltpu.make_async_copy(
                act_hbm.at[pl.ds(pl.multiple_of(owner * B, B), B)], act.at[q], load_sem.at[6 + q]
            )
        )
    for copy in loads:
        copy.start()

    barrier = pltpu.get_barrier_semaphore()
    everyone = [zdev[1], zdev[-1], xdev, cdev, sdev] + ydev
    for dev in everyone:
        pl.semaphore_signal(barrier, inc=1, device_id=dev, device_id_type=MESH)
    pl.semaphore_wait(barrier, len(everyone))

    sent = []

    def start(copy):
        copy.start()
        sent.append(copy)

    def flush():
        for copy in sent:
            copy.wait_send()
        sent.clear()

    tokens = (xs, us)

    def gz(t, i):
        direction, here, half, there = GZ[i]
        return remote(
            tokens[t].at[pl.ds(row(here, 0, half), B)], tokens[t].at[pl.ds(row(there, 0, half), B)],
            gz_s.at[t, i], gz_r.at[t, i], zdev[direction],
        )

    def gx(t, d):
        i = GX.index(d)
        return remote(
            tokens[t].at[pl.ds(row(d, 0, 0), B)], tokens[t].at[pl.ds(row(d, 0, 1), B)],
            gx_s.at[t, i], gx_r.at[t, i], xdev,
        )

    def gc(t, d):
        return remote(
            tokens[t].at[pl.ds(row(d, 0, 0), 2 * B)], tokens[t].at[pl.ds(row(d, 1, 0), 2 * B)],
            gc_s.at[t, d], gc_r.at[t, d], cdev,
        )

    def got_z(t, d, half):
        gz(t, GZ_INTO[d, half]).wait_recv()

    def got_x(t, d):
        gx(t, d).wait_recv()

    def gather(t, step):
        if step == 0:
            loads[t].wait()
            start(gz(t, 0))
            start(gz(t, 1))
            start(gx(t, 0))
        elif step == 1:
            got_z(t, 1, 0)
            start(gz(t, 2))
            start(gx(t, 1))
            got_z(t, 7, 0)
            start(gz(t, 3))
            start(gx(t, 7))
            got_x(t, 0)
            start(gc(t, 0))
        elif step == 2:
            got_z(t, 2, 0)
            start(gz(t, 4))
            start(gx(t, 2))
            got_z(t, 6, 0)
            start(gz(t, 5))
            start(gx(t, 6))
            got_x(t, 1)
            start(gc(t, 1))
            got_x(t, 7)
            start(gc(t, 7))
        elif step == 3:
            got_z(t, 3, 0)
            start(gz(t, 6))
            got_x(t, 2)
            start(gz(t, 7))
            start(gc(t, 2))
            got_z(t, 5, 0)
            got_x(t, 6)
            start(gz(t, 8))
            start(gc(t, 6))
        elif step == 4:
            got_z(t, 5, 1)
            start(gz(t, 9))
            start(gc(t, 5))
            got_z(t, 3, 1)
            start(gc(t, 3))
        else:
            got_z(t, 4, 0)
            got_z(t, 4, 1)
            start(gc(t, 4))

    result = (lat, pre)

    def ry(t, q, k):
        return remote(
            part.at[t, pl.ds(pl.multiple_of(q * CH + ypos[k] * 64, 64), 64)], yin.at[t, q, k],
            ry_s.at[t, q, k], ry_r.at[t, q, k], ydev[k],
        )

    def rx(t, q):
        return remote(xout.at[t, q], xin.at[t, q], rx_s.at[t, q], rx_r.at[t, q], sdev)

    def ax(t, q):
        rows = pl.ds(pl.multiple_of(q * CH + s * B, B), B)
        return remote(result[t].at[rows], result[t].at[rows], ax_s.at[t, q], ax_r.at[t, q], sdev)

    def ay(t, q, k):
        rows = pl.ds(pl.multiple_of(q * CH + y * 64, 64), 64)
        return remote(result[t].at[rows], result[t].at[rows], ay_s.at[t, q, k], ay_r.at[t, q, k], ydev[k])

    def sec_a(t, q):
        for d in PAIRS[q]:
            gc(t, d).wait_recv()
        rows = pl.ds(q * CH, CH)
        if t == 0:
            acc = jnp.dot(xs[rows], we[...], preferred_element_type=F32)
        else:
            acc = lax.dot_general(us[rows], wd[...], (((1,), (1,)), ((), ())), preferred_element_type=F32)
        full[...] = acc
        part[t, rows] = acc.astype(BF16)
        for k in (1, 0, 2):
            start(ry(t, q, k))
        own[t, q] = full[pl.ds(pl.multiple_of(y * 64, 64), 64)]

    def sec_b(t, q):
        for k in range(3):
            ry(t, q, k).wait_recv()
        own[t, q] = (
            own[t, q] + yin[t, q, 0].astype(F32) + yin[t, q, 1].astype(F32) + yin[t, q, 2].astype(F32)
        )
        xout[t, q] = own[t, q, pl.ds(pl.multiple_of((1 - xl) * B, B), B)]
        start(rx(t, q))

    def sec_c(t, q):
        rx(t, q).wait_recv()
        total = own[t, q, pl.ds(pl.multiple_of(xl * B, B), B)] + xin[t, q]
        if t == 0:
            total = total + be[...]
        value = (act[q].astype(F32) * total).astype(BF16)
        result[t][pl.ds(pl.multiple_of(q * CH + s * B, B), B)] = value
        start(ax(t, q))

    def sec_d(t, q):
        ax(t, q).wait_recv()
        for k in (1, 0, 2):
            start(ay(t, q, k))

    def sec_e(t, q):
        for k in range(3):
            ay(t, q, k).wait_recv()

    def dc(d):
        return remote(dec.at[pl.ds(row(d, 1, 0), 2 * B)], cin.at[d], dc_s.at[d], dc_r.at[d], cdev)

    def decode(q):
        sec_e(0, q)

        @pl.loop(0, 4)
        def _(n):
            cols = pl.ds(pl.multiple_of(n * 512, 512), 512)
            dec[pl.ds(q * CH, CH), cols] = jnp.dot(
                lat[pl.ds(q * CH, CH)], wd[:, cols], preferred_element_type=F32
            )

        for d in PAIRS[q]:
            start(dc(d))

    def rz(i):
        return remote(stage.at[i], zin.at[i], rz_s.at[i], rz_r.at[i], zdev[RZ[i][0]])

    def xr(i):
        return remote(stage.at[10 + i], xrin.at[i], xr_s.at[i], xr_r.at[i], xdev)

    def total(d, half, cols):
        value = dec[pl.ds(row(d, 0, half), B), cols] + cin[d, pl.ds(half * B, B), cols]
        for i in rz_into(d, half):
            value = value + zin[i, :, cols].astype(F32)
        if half == 0 and d in GX:
            value = value + xrin[GX.index(d), :, cols].astype(F32)
        return value

    def arrived(d, half):
        for i in rz_into(d, half):
            rz(i).wait_recv()
        if half == 0 and d in GX:
            xr(GX.index(d)).wait_recv()

    def reduce(d, half):
        arrived(d, half)
        i = RZ_OF.get((d, half))
        slot = 10 + GX.index(d) if i is None else i

        @pl.loop(0, 4)
        def _(n):
            cols = pl.ds(pl.multiple_of(n * 512, 512), 512)
            stage[slot, :, cols] = total(d, half, cols).astype(BF16)

        start(xr(slot - 10) if i is None else rz(i))

    def finish():
        arrived(0, 0)

        @pl.loop(0, 4)
        def _(n):
            cols = pl.ds(pl.multiple_of(n * 512, 512), 512)
            reb[:, cols] = (total(0, 0, cols) + bd[:, cols]).astype(BF16)

        copy = pltpu.make_async_copy(reb, reb_hbm, store_sem.at[0])
        copy.start()
        return copy

    def dec_grad(n):
        cols = pl.ds(n * 512, 512)
        gd[:, cols] = lax.dot_general(
            lat[...], us[:, cols], (((0,), (0,)), ((), ())), preferred_element_type=F32
        ).astype(BF16)

    def enc_grad(n):
        @pl.loop(0, 4)
        def _(m):
            at = n * 1024 + m * 256
            rows = pl.ds(pl.multiple_of(at, 256), 256)
            ge[rows] = lax.dot_general(
                xs[:, rows], pre[...], (((0,), (0,)), ((), ())), preferred_element_type=F32
            ).astype(BF16)

        rows = pl.ds(n * 1024, 1024)
        copy = pltpu.make_async_copy(ge.at[rows], ge_hbm.at[rows], store_sem.at[2 + n])
        copy.start()
        return copy

    gather(0, 0)
    gather(0, 1)
    gather(1, 0)
    gather(0, 2)
    loads[2].wait()
    sec_a(0, 0)
    gather(1, 1)
    gather(0, 3)
    sec_a(0, 1)
    gather(1, 2)
    sec_b(0, 0)
    gather(0, 4)
    sec_a(0, 2)
    for copy in loads[3:]:
        copy.wait()
    gather(1, 3)
    sec_a(1, 0)
    sec_b(0, 1)
    sec_c(0, 0)
    gather(0, 5)
    sec_a(0, 3)
    gather(1, 4)
    sec_a(1, 1)
    sec_b(0, 2)
    sec_c(0, 1)
    sec_d(0, 0)
    sec_b(1, 0)
    gather(1, 5)
    sec_b(0, 3)
    sec_c(0, 2)
    sec_d(0, 1)
    sec_a(1, 2)
    sec_c(0, 3)
    sec_d(0, 2)
    sec_b(1, 1)
    sec_c(1, 0)
    sec_d(0, 3)
    sec_a(1, 3)
    decode(0)
    decode(1)
    sec_b(1, 2)
    sec_c(1, 1)
    sec_d(1, 0)
    decode(2)
    sec_b(1, 3)
    decode(3)
    for d in range(8):
        dc(d).wait_recv()
    for unit in ((4, 0), (4, 1), (3, 1), (5, 0), (1, 1), (7, 1), (0, 1)):
        reduce(*unit)
    sec_c(1, 2)
    sec_d(1, 1)
    sec_c(1, 3)
    reduce(3, 0)
    reduce(5, 1)
    sec_d(1, 2)
    sec_d(1, 3)
    dec_grad(0)
    reduce(2, 1)
    reduce(6, 1)
    dec_grad(1)
    dec_grad(2)
    reduce(2, 0)
    reduce(6, 0)
    dec_grad(3)
    stores = [pltpu.make_async_copy(gd, gd_hbm, store_sem.at[1])]
    stores[0].start()
    for q in range(4):
        sec_e(1, q)
    reduce(1, 0)
    reduce(7, 0)
    stores.append(enc_grad(0))
    stores.append(finish())
    stores.append(enc_grad(1))
    flush()
    for copy in stores:
        copy.wait()


def per_device(stacked, enc_weight, enc_bias, dec_weight, dec_bias, active, upstream):
    hbm = pl.BlockSpec(memory_space=pl.ANY)
    dma = pltpu.SemaphoreType.DMA
    return pl.pallas_call(
        kernel,
        out_shape=(
            jax.ShapeDtypeStruct((B, FEAT), BF16),
            jax.ShapeDtypeStruct((FEAT, LATS), BF16),
            jax.ShapeDtypeStruct((LATS, FEAT), BF16),
        ),
        in_specs=[hbm] * 7,
        out_specs=(hbm,) * 3,
        scratch_shapes=[
            pltpu.VMEM((TOK, FEAT), BF16),
            pltpu.VMEM((TOK, FEAT), BF16),
            pltpu.VMEM((FEAT, LATS), BF16),
            pltpu.VMEM((LATS, FEAT), BF16),
            pltpu.VMEM((1, LATS), F32),
            pltpu.VMEM((1, FEAT), F32),
            pltpu.VMEM((4, B, LATS), jnp.int32),
            pltpu.VMEM((2, TOK, LATS), BF16),
            pltpu.VMEM((CH, LATS), F32),
            pltpu.VMEM((2, 4, 64, LATS), F32),
            pltpu.VMEM((2, 4, 3, 64, LATS), BF16),
            pltpu.VMEM((2, 4, B, LATS), F32),
            pltpu.VMEM((2, 4, B, LATS), F32),
            pltpu.VMEM((TOK, LATS), BF16),
            pltpu.VMEM((TOK, LATS), BF16),
            pltpu.VMEM((TOK, FEAT), F32),
            pltpu.VMEM((8, 2 * B, FEAT), F32),
            pltpu.VMEM((15, B, FEAT), BF16),
            pltpu.VMEM((10, B, FEAT), BF16),
            pltpu.VMEM((5, B, FEAT), BF16),
            pltpu.VMEM((FEAT, LATS), BF16),
            pltpu.VMEM((LATS, FEAT), BF16),
            pltpu.VMEM((B, FEAT), BF16),
            dma((10,)), dma((4,)),
            dma((2, 10)), dma((2, 10)), dma((2, 5)), dma((2, 5)), dma((2, 8)), dma((2, 8)),
            dma((2, 4, 3)), dma((2, 4, 3)), dma((2, 4)), dma((2, 4)),
            dma((2, 4)), dma((2, 4)), dma((2, 4, 3)), dma((2, 4, 3)),
            dma((8,)), dma((8,)), dma((10,)), dma((10,)), dma((5,)), dma((5,)),
        ],
        compiler_params=pltpu.CompilerParams(
            collective_id=0, has_side_effects=True, vmem_limit_bytes=58 << 20
        ),
        cost_estimate=pl.CostEstimate(flops=10 * 1024 * 2048 * 512, bytes_accessed=14 << 20, transcendentals=0),
    )(
        stacked, enc_weight, enc_bias.reshape(1, -1), dec_weight, dec_bias.reshape(1, -1), active, upstream
    )


def solution(mesh):
    placed = (
        P("lat", "section"),
        P("section", "lat"),
        P("lat"),
        P("lat", "section"),
        P("section"),
        P(None, "lat"),
        P("lat", "section"),
    )
    return jax.shard_map(
        per_device,
        mesh=mesh,
        in_specs=placed,
        out_specs=(P("lat", "section"), P("section", "lat"), P("lat", "section")),
        check_vma=False,
    )
```

time: 550 us -> 115 us (0.21)
  waiting for transfers between devices: 496 us -> 0 us
  Pallas kernels: 0 us -> 106 us
  matrix products: 31.3 us -> 0 us
  between operations: 13.8 us -> 0.64 us
    psum x1 -> x0, waiting for transfers between devices: 184 us -> none  [per_device(): preact = lax.psum(partial_value, 'section') + enc_bias]
    all_gather x2 -> x0, waiting for transfers between devices: 172 us -> none  [the longest x1 91.8 us: per_device(): upstream_all = lax.all_gather(upstream, 'lat', axis=0, tiled=True)]
    reduce_scatter x1 -> x0, waiting for transfers between devices: 138 us -> none  [per_device(): lax.psum_scatter(jnp.dot(latent, dec_weight, preferred_element_type=jnp.f...]
    pallas_call x0 -> x1, Pallas kernels: none -> 106 us  [per_device(): pl.pallas_call(kernel, out_shape=(jax.ShapeDtypeStruct((B, FEAT), BF16),...]
    dot_general x5 -> x0, matrix products: 31.3 us -> none  [the longest x1 7.34 us: per_device(): lax.dot_general(stacked_all, pre_grad, (((0,), (0,)), ((), ())), preferre...]
  transfers between devices with their start and end apart: 4 -> 0, of which waited for: 4 -> 0; matrix products, arithmetic and copies ran while one was open for 4% -> 0% of each run, Pallas kernels for 0% -> 0%
where the time goes in v1:
time: 115 us; the launch traced here: 113 us
  Pallas kernels  106 us (92%)
  local copies, waits for them, and re-layouts  6.08 us (5%)
    pallas_call x1, Pallas kernels, per_device(): pl.pallas_call(kernel, out_shape=(jax.ShapeDtypeStruct((B, FEAT), BF16),...  106 us
    unnamed x5, local copies, waits for them, and re-layouts  6.08 us

profile of v1, /device:TPU:8, one launch (start us, length us, event | category | flops | bytes accessed | tf_op | source)
XLA Modules:
  0.0 113.1 jit_solution(8955265957430535763)
XLA Ops:
  0.6 106.4 %shard_map.94 = (bf16[32,2048]{1,0:T(8,128)(2,1)}, bf16[2048,512]{1,0:T(8,128)(2,1)}, bf16[512,2048]{1,0:T(8,128)(2,1)}) custom-call(bf16[32,2048]{1,0:T(8,128)(2,1)} %x_hbm.1, bf16[2048,512]{1,0:T(8,128)(2,1)} %we_hbm.1, f32[1,512]{1,0:T(1,128)} %bitcast.3, bf16[512,2048]{1,0:T(8,128)(2,1)} %wd_hbm.1, f32[1,2048]{1,0:T(1,128)} %bitcast.2, ...), custom_call_target="tpu_custom_call" | custom-call | flops 10737418240 | bytes 14680064 | tf_op jit(solution)/shard_map/pallas_call | solution.py:412
  107.0 1.6 %copy.13 = bf16[32,2048]{1,0:T(8,128)(2,1)} copy(bf16[32,2048]{1,0:T(8,128)(2,1)} %get-tuple-element.6) | data formatting | bytes 262144
  108.6 0.0 copy-start
  108.6 3.2 %copy.14 = bf16[2048,512]{1,0:T(8,128)(2,1)} copy(bf16[2048,512]{1,0:T(8,128)(2,1)} %get-tuple-element.7) | data formatting | bytes 4194304
  111.8 0.0 copy-done
  111.8 1.3 %copy.15 = bf16[512,2048]{1,0:T(8,128)(2,1)} copy(bf16[512,2048]{1,0:T(8,128)(2,1)S(1)} %copy-done) | data formatting | bytes 4194304
Async XLA Ops:
  108.6 3.2 %copy-start = (bf16[512,2048]{1,0:T(8,128)(2,1)S(1)}, bf16[512,2048]{1,0:T(8,128)(2,1)}, u32[]{:S(2)}) copy-start(bf16[512,2048]{1,0:T(8,128)(2,1)} %get-tuple-element.8) | copy-start | bytes 6291460

commit v2 on v0

v2 whole, which is shorter than its diff:
```python
import jax
import jax.numpy as jnp
from jax import lax
from jax.experimental import pallas as pl
from jax.experimental.pallas import tpu as pltpu
from jax.sharding import PartitionSpec as P

F32, BF16 = jnp.float32, jnp.bfloat16
MESH = pl.DeviceIdType.MESH
B = 32
H = 16
FEAT = 2048
LATS = 512
TOK = 1024
CH = 256

PLACE = {1: 0, 7: 1, 2: 2, 6: 3, 3: 4, 5: 5, 0: 6, 4: 7}
PAIRS = ((1, 7), (2, 6), (3, 5), (0, 4))


def row(a, d, core, half):
    group, place = divmod(PLACE[d], 4)
    return a * 512 + group * CH + core * 128 + place * 32 + half * H


SPREAD_X = (
    (None, "z", -1, (0, 0), (1, 0)), (None, "z", 1, (0, 0), (7, 0)), (None, "x", 0, (0, 0), (0, 1)),
    (None, "z", -1, (1, 0), (2, 0)), (None, "z", 1, (7, 0), (6, 0)), (None, "x", 0, (1, 0), (1, 1)),
    (None, "x", 0, (7, 0), (7, 1)), (None, "z", -1, (2, 0), (3, 0)), (None, "z", 1, (6, 0), (5, 0)),
    (None, "x", 0, (2, 0), (2, 1)), (None, "x", 0, (6, 0), (6, 1)), (0, "z", -1, (3, 0), (4, 0)),
    (1, "z", 1, (5, 0), (4, 0)), (None, "z", -1, (2, 1), (3, 1)), (None, "z", 1, (6, 1), (5, 1)),
    (None, "x", 0, (4, 0), (4, 1)),
)
SPREAD_UP = (
    (None, "z", -1, (0, 0), (1, 0)), (None, "z", 1, (0, 0), (7, 0)), (None, "x", 0, (0, 0), (0, 1)),
    (None, "z", -1, (1, 0), (2, 0)), (None, "z", 1, (7, 0), (6, 0)), (None, "x", 0, (1, 0), (1, 1)),
    (None, "x", 0, (7, 0), (7, 1)), (None, "z", -1, (2, 0), (3, 0)), (None, "z", 1, (6, 0), (5, 0)),
    (None, "z", -1, (1, 1), (2, 1)), (None, "z", 1, (7, 1), (6, 1)), (0, "z", -1, (3, 0), (4, 0)),
    (1, "z", 1, (5, 0), (4, 0)), (None, "z", -1, (2, 1), (3, 1)), (None, "z", 1, (6, 1), (5, 1)),
    (0, "z", 1, (5, 1), (4, 1)), (1, "z", -1, (3, 1), (4, 1)),
)
SPREAD = (SPREAD_X, SPREAD_UP)
SUM = (
    (1, "z", 2, (4, 1), (2, 1)), (0, "z", -2, (4, 1), (6, 1)), (None, "z", -1, (5, 1), (6, 1)),
    (None, "z", 1, (3, 1), (2, 1)), (None, "x", 0, (7, 1), (7, 0)), (None, "x", 0, (1, 1), (1, 0)),
    (None, "z", -1, (5, 0), (6, 0)), (None, "z", 1, (3, 0), (2, 0)), (None, "x", 0, (6, 1), (6, 0)),
    (None, "x", 0, (2, 1), (2, 0)), (1, "z", -2, (4, 0), (6, 0)), (0, "z", 2, (4, 0), (2, 0)),
    (None, "x", 0, (0, 1), (0, 0)), (None, "z", -1, (7, 0), (0, 0)), (None, "z", 1, (1, 0), (0, 0)),
    (None, "z", -2, (6, 0), (0, 0)), (None, "z", 2, (2, 0), (0, 0)),
)

def leaving(table, a, block):
    return [i for i, (part, _, _, here, _) in enumerate(table) if part in (None, a) and here == block]


def coming(table, a, block):
    return [i for i, (part, _, _, _, there) in enumerate(table) if part in (None, a) and there == block]


PLAN = (
    ("take", 0, 0, 0, 0), ("take", 0, 1, 0, 0), ("take", 0, 0, 1, 0), ("take", 0, 0, 7, 0), ("ready", 4, 5),
    ("ready", 5, 8), ("take", 0, 0, 0, 1), ("ready", 8, 24), ("take", 0, 1, 1, 0), ("take", 0, 1, 7, 0),
    ("take", 0, 1, 0, 1), ("take", 0, 0, 2, 0), ("take", 0, 0, 6, 0), ("take", 0, 0, 1, 1),
    ("take", 0, 1, 2, 0), ("take", 0, 1, 6, 0), ("take", 0, 0, 7, 1), ("share", 0, 0, 0),
    ("take", 0, 1, 1, 1), ("take", 0, 0, 3, 0), ("take", 0, 0, 5, 0), ("take", 0, 1, 7, 1),
    ("share", 0, 1, 0), ("take", 0, 1, 3, 0), ("take", 0, 1, 5, 0), ("take", 0, 0, 2, 1),
    ("take", 0, 0, 4, 0), ("take", 0, 0, 6, 1), ("share", 0, 0, 1), ("take", 0, 1, 4, 0),
    ("take", 0, 1, 2, 1), ("take", 1, 0, 0, 0), ("sec_a", 0, 0), ("take", 0, 0, 3, 1), ("take", 0, 1, 6, 1),
    ("share", 0, 1, 1), ("take", 1, 1, 0, 0), ("take", 0, 0, 5, 1), ("share", 0, 0, 2), ("take", 0, 0, 4, 1),
    ("share", 0, 0, 3), ("sec_a", 0, 2), ("take", 0, 1, 3, 1), ("take", 0, 1, 4, 1), ("share", 0, 1, 3),
    ("take", 1, 0, 7, 0), ("sec_a", 0, 1), ("take", 0, 1, 5, 1), ("share", 0, 1, 2), ("take", 1, 0, 0, 1),
    ("take", 1, 0, 1, 0), ("take", 1, 1, 1, 0), ("sec_b", 0, 0), ("take", 1, 1, 0, 1), ("take", 1, 1, 7, 0),
    ("sec_a", 0, 3), ("take", 1, 0, 6, 0), ("take", 1, 0, 7, 1), ("sec_b", 0, 2), ("take", 1, 0, 2, 0),
    ("take", 1, 0, 1, 1), ("share", 1, 0, 0), ("take", 1, 1, 6, 0), ("take", 1, 1, 2, 0),
    ("take", 1, 1, 1, 1), ("sec_b", 0, 1), ("take", 1, 0, 5, 0), ("sec_c", 0, 0), ("take", 1, 0, 3, 0),
    ("take", 1, 0, 6, 1), ("take", 1, 1, 7, 1), ("share", 1, 1, 0), ("sec_c", 0, 2), ("sec_b", 0, 3),
    ("take", 1, 0, 2, 1), ("take", 1, 1, 5, 0), ("share", 1, 0, 1), ("sec_c", 0, 1), ("take", 1, 1, 3, 0),
    ("take", 1, 0, 5, 1), ("sec_a", 1, 0), ("decode", 0), ("sec_c", 0, 3), ("take", 1, 0, 4, 0),
    ("take", 1, 1, 2, 1), ("take", 1, 1, 6, 1), ("take", 1, 1, 4, 0), ("share", 1, 1, 1),
    ("take", 1, 0, 3, 1), ("share", 1, 0, 2), ("decode", 2), ("collect", 0, 0), ("reduce", 0, 1, 1),
    ("reduce", 0, 7, 1), ("take", 1, 0, 4, 1), ("share", 1, 0, 3), ("collect", 0, 1), ("decode", 1),
    ("take", 1, 1, 3, 1), ("take", 1, 1, 5, 1), ("sec_a", 1, 2), ("collect", 2, 0), ("reduce", 1, 1, 1),
    ("reduce", 1, 7, 1), ("share", 1, 1, 2), ("reduce", 0, 1, 0), ("sec_b", 1, 0), ("collect", 2, 1),
    ("sec_a", 1, 1), ("reduce", 0, 7, 0), ("take", 1, 1, 4, 1), ("share", 1, 1, 3), ("collect", 1, 0),
    ("reduce", 0, 3, 1), ("reduce", 0, 5, 1), ("reduce", 0, 3, 0), ("reduce", 0, 5, 0), ("decode", 3),
    ("reduce", 1, 1, 0), ("collect", 1, 1), ("reduce", 0, 4, 1), ("reduce", 0, 4, 0), ("reduce", 0, 0, 1),
    ("sec_a", 1, 3), ("reduce", 1, 7, 0), ("reduce", 0, 2, 1), ("sec_c", 1, 0), ("collect", 3, 0),
    ("reduce", 1, 3, 1), ("reduce", 1, 5, 1), ("reduce", 1, 3, 0), ("reduce", 1, 5, 0), ("sec_b", 1, 2),
    ("collect", 3, 1), ("reduce", 1, 4, 1), ("reduce", 1, 4, 0), ("reduce", 1, 0, 1), ("sec_b", 1, 1),
    ("dec_grad", 0), ("dec_grad", 1), ("reduce", 0, 6, 1), ("reduce", 0, 2, 0), ("sec_b", 1, 3),
    ("sec_c", 1, 2), ("dec_grad", 2), ("dec_grad", 3), ("sec_c", 1, 1), ("reduce", 1, 6, 1), ("sec_e", 1, 0),
    ("reduce", 0, 6, 0), ("sec_c", 1, 3), ("reduce", 1, 2, 1), ("sec_e", 1, 2), ("reduce", 1, 6, 0),
    ("sec_e", 1, 1), ("finish", 0), ("reduce", 1, 2, 0), ("sec_e", 1, 3), ("enc_grad", 0), ("enc_grad", 1),
    ("enc_grad", 2), ("finish", 1), ("enc_grad", 3),
)

def kernel(
    x_hbm, we_hbm, be_hbm, wd_hbm, bd_hbm, act_hbm, up_hbm,
    reb_hbm, ge_hbm, gd_hbm,
    xs, us, we, wd, be, bd, act,
    part, full, own, yin, xout, xin, lat, pre,
    dec, cin, stage, sums_in, ge, gd, reb,
    load_sem, store_sem, g_s, g_r, gc_s, gc_r,
    ry_s, ry_r, rx_s, rx_r, ay_s, ay_r, dc_s, dc_r, s_s, s_r,
):
    s = lax.axis_index("section")
    l = lax.axis_index("lat")
    y, xl = s // 2, lax.rem(s, 2)
    xh, z, c = l // 16, lax.rem(l, 16) // 2, lax.rem(l, 2)

    def at_lat(h, zz, cc):
        return h * 16 + zz * 2 + cc

    zdev = {step: (s, at_lat(xh, lax.rem(z + step + 8, 8), c)) for step in (-2, -1, 1, 2)}
    xdev = (s, at_lat(1 - xh, z, c))
    cdev = (s, at_lat(xh, z, 1 - c))
    ypos = [lax.rem(y + k, 4) for k in (1, 2, 3)]
    ydev = [(p * 2 + xl, l) for p in ypos]
    sdev = (y * 2 + 1 - xl, l)

    def remote(src, dst, sems, at, dev):
        return pltpu.make_async_remote_copy(
            src_ref=src, dst_ref=dst, send_sem=sems[0].at[at], recv_sem=sems[1].at[at], device_id=dev,
            device_id_type=MESH,
        )

    loads = [
        pltpu.make_async_copy(hbm.at[pl.ds(a * H, H)], ref.at[pl.ds(row(a, 0, 0, 0), H)], load_sem.at[t, a])
        for t, (hbm, ref) in enumerate(((x_hbm, xs), (up_hbm, us)))
        for a in (0, 1)
    ]
    loads += [
        pltpu.make_async_copy(we_hbm, we, load_sem.at[2, 0]),
        pltpu.make_async_copy(wd_hbm, wd, load_sem.at[2, 1]),
        pltpu.make_async_copy(be_hbm, be, load_sem.at[3, 0]),
        pltpu.make_async_copy(bd_hbm, bd, load_sem.at[3, 1]),
    ]
    score, other = y // 2, lax.rem(y, 2)
    for q in range(4):
        a, group = divmod(q, 2)
        for n in range(4):
            odd, half = divmod(n, 2)
            dist = (1 - other) * (3 - 6 * odd) + other * 4 * odd if group else (other + 1) * (1 - 2 * odd)
            owner = at_lat(lax.rem(xh + half, 2), lax.rem(z + dist + 8, 8), lax.rem(c + score, 2))
            loads.append(
                pltpu.make_async_copy(
                    act_hbm.at[pl.ds(pl.multiple_of(owner * B + a * H, H), H)],
                    act.at[q, pl.ds(n * H, H)], load_sem.at[4 + q, n],
                )
            )
    for copy in loads:
        copy.start()

    barrier = pltpu.get_barrier_semaphore()
    everyone = list(zdev.values()) + [xdev, cdev, sdev] + ydev
    for dev in everyone:
        pl.semaphore_signal(barrier, inc=1, device_id=dev, device_id_type=MESH)
    pl.semaphore_wait(barrier, len(everyone))

    sent = []

    def start(copy):
        copy.start()
        sent.append(copy)

    stores = []

    def store(copy):
        copy.start()
        stores.append(copy)

    def flush():
        for copy in sent:
            copy.wait_send()
        sent.clear()

    tokens = (xs, us)

    def spread(t, a, i):
        _, axis, step, here, there = SPREAD[t][i]
        return remote(
            tokens[t].at[pl.ds(row(a, here[0], 0, here[1]), H)], tokens[t].at[pl.ds(row(a, there[0], 0, there[1]), H)],
            (g_s, g_r), (t, a, i), xdev if axis == "x" else zdev[step],
        )

    def gc(t, a, p):
        d = PAIRS[p][0]
        return remote(
            tokens[t].at[pl.ds(row(a, d, 0, 0), 4 * H)], tokens[t].at[pl.ds(row(a, d, 1, 0), 4 * H)],
            (gc_s, gc_r), (t, a, p), cdev,
        )

    def take(t, a, d, half):
        if (d, half) == (0, 0):
            loads[2 * t + a].wait()
        for i in coming(SPREAD[t], a, (d, half)):
            spread(t, a, i).wait_recv()
        for i in leaving(SPREAD[t], a, (d, half)):
            start(spread(t, a, i))

    def share(t, a, p):
        start(gc(t, a, p))

    result = (lat, pre)

    def ry(t, q, k):
        return remote(
            part.at[t, pl.ds(pl.multiple_of(q * CH + ypos[k] * 64, 64), 64)], yin.at[t, q, k],
            (ry_s, ry_r), (t, q, k,), ydev[k],
        )

    def rx(t, q):
        return remote(xout.at[t, q], xin.at[t, q], (rx_s, rx_r), (t, q), sdev)

    def ay(t, q, k):
        rows = pl.ds(pl.multiple_of(q * CH + y * 64, 64), 64)
        return remote(result[t].at[rows], result[t].at[rows], (ay_s, ay_r), (t, q, k,), ydev[k])

    def sec_a(t, q):
        a, group = divmod(q, 2)
        gc(t, a, 2 * group).wait_recv()
        gc(t, a, 2 * group + 1).wait_recv()
        rows = pl.ds(q * CH, CH)
        if t == 0:
            acc = jnp.dot(xs[rows], we[...], preferred_element_type=F32)
        else:
            acc = lax.dot_general(us[rows], wd[...], (((1,), (1,)), ((), ())), preferred_element_type=F32)
        full[...] = acc
        part[t, rows] = acc.astype(BF16)
        for k in (1, 0, 2):
            start(ry(t, q, k))
        own[t, q] = full[pl.ds(pl.multiple_of(y * 64, 64), 64)]

    def sec_b(t, q):
        for k in range(3):
            ry(t, q, k).wait_recv()
        own[t, q] = (
            own[t, q] + yin[t, q, 0].astype(F32) + yin[t, q, 1].astype(F32) + yin[t, q, 2].astype(F32)
        )
        xout[t, q] = own[t, q].astype(BF16)
        start(rx(t, q))

    def sec_c(t, q):
        rx(t, q).wait_recv()
        total = own[t, q] + xin[t, q].astype(F32)
        if t == 0:
            total = total + be[...]
        value = (act[q].astype(F32) * total).astype(BF16)
        result[t][pl.ds(pl.multiple_of(q * CH + y * 64, 64), 64)] = value
        for k in (1, 0, 2):
            start(ay(t, q, k))

    def sec_e(t, q):
        for k in range(3):
            ay(t, q, k).wait_recv()

    def dc(q, p):
        rows = pl.ds(q * CH + 128 + p * 64, 64)
        return remote(dec.at[rows], cin.at[q, pl.ds(p * 64, 64)], (dc_s, dc_r), (q, p), cdev)

    def decode(q):
        sec_e(0, q)

        @pl.loop(0, 4)
        def _(n):
            cols = pl.ds(pl.multiple_of(n * 512, 512), 512)
            dec[pl.ds(q * CH, CH), cols] = jnp.dot(
                lat[pl.ds(q * CH, CH)], wd[:, cols], preferred_element_type=F32
            )

        start(dc(q, 0))
        start(dc(q, 1))

    def summed(a, i):
        _, axis, step, _, _ = SUM[i]
        return remote(
            stage.at[a, i], sums_in.at[a, i], (s_s, s_r), (a, i), xdev if axis == "x" else zdev[step]
        )

    def total(a, d, half, cols):
        group, place = divmod(PLACE[d], 4)
        value = dec[pl.ds(row(a, d, 0, half), H), cols] + cin[2 * a + group, pl.ds(place * 32 + half * H, H), cols]
        for i in coming(SUM, a, (d, half)):
            value = value + sums_in[a, i, :, cols].astype(F32)
        return value

    def collect(q, p):
        dc(q, p).wait_recv()

    def arrived(a, d, half):
        for i in coming(SUM, a, (d, half)):
            summed(a, i).wait_recv()

    def reduce(a, d, half):
        arrived(a, d, half)
        (i,) = leaving(SUM, a, (d, half))

        @pl.loop(0, 2)
        def _(n):
            cols = pl.ds(pl.multiple_of(n * 1024, 1024), 1024)
            stage[a, i, :, cols] = total(a, d, half, cols).astype(BF16)

        start(summed(a, i))

    def finish(a):
        arrived(a, 0, 0)
        rows = pl.ds(a * H, H)

        @pl.loop(0, 2)
        def _(n):
            cols = pl.ds(pl.multiple_of(n * 1024, 1024), 1024)
            reb[rows, cols] = (total(a, 0, 0, cols) + bd[:, cols]).astype(BF16)

        store(pltpu.make_async_copy(reb.at[rows], reb_hbm.at[rows], store_sem.at[a]))

    def dec_grad(n):
        cols = pl.ds(n * 512, 512)
        gd[:, cols] = lax.dot_general(
            lat[...], us[:, cols], (((0,), (0,)), ((), ())), preferred_element_type=F32
        ).astype(BF16)
        if n == 3:
            store(pltpu.make_async_copy(gd, gd_hbm, store_sem.at[2]))

    def enc_grad(n):
        for m in (0, 1):
            rows = pl.ds(n * 512 + m * 256, 256)
            ge[rows] = lax.dot_general(
                xs[:, rows], pre[...], (((0,), (0,)), ((), ())), preferred_element_type=F32
            ).astype(BF16)
        rows = pl.ds(n * 512, 512)
        store(pltpu.make_async_copy(ge.at[rows], ge_hbm.at[rows], store_sem.at[3 + n]))

    def ready(first, last):
        for i in range(first, last):
            loads[i].wait()

    phases = {
        f.__name__: f
        for f in (
            ready, take, share, sec_a, sec_b, sec_c, sec_e, decode, collect, reduce, finish, dec_grad, enc_grad
        )
    }
    plan = [(phases[name], args) for name, *args in PLAN]
    for phase, args in plan:
        phase(*args)
    flush()
    for copy in stores:
        copy.wait()


def copy_out(reb, ge, gd, reb_out, ge_out, gd_out, reb_v, ge_v, gd_v, sems):
    pieces = [(reb, reb_v, reb_out, pl.ds(0, B))]
    for src, held, dst in ((ge, ge_v, ge_out), (gd, gd_v, gd_out)):
        step = src.shape[0] // 4
        pieces += [(src, held, dst, pl.ds(n * step, step)) for n in range(4)]
    ins = [
        pltpu.make_async_copy(src.at[rows], held.at[rows], sems.at[0, n])
        for n, (src, held, _, rows) in enumerate(pieces)
    ]
    outs = [
        pltpu.make_async_copy(held.at[rows], dst.at[rows], sems.at[1, n])
        for n, (_, held, dst, rows) in enumerate(pieces)
    ]
    for copy in ins:
        copy.start()
    for arriving, leaving in zip(ins, outs):
        arriving.wait()
        leaving.start()
    for copy in outs:
        copy.wait()


def per_device(stacked, enc_weight, enc_bias, dec_weight, dec_bias, active, upstream):
    hbm = pl.BlockSpec(memory_space=pl.ANY)
    dma = pltpu.SemaphoreType.DMA
    shapes = (
        jax.ShapeDtypeStruct((B, FEAT), BF16),
        jax.ShapeDtypeStruct((FEAT, LATS), BF16),
        jax.ShapeDtypeStruct((LATS, FEAT), BF16),
    )
    outs = pl.pallas_call(
        kernel,
        out_shape=shapes,
        in_specs=[hbm] * 7,
        out_specs=(hbm,) * 3,
        scratch_shapes=[
            pltpu.VMEM((TOK, FEAT), BF16),
            pltpu.VMEM((TOK, FEAT), BF16),
            pltpu.VMEM((FEAT, LATS), BF16),
            pltpu.VMEM((LATS, FEAT), BF16),
            pltpu.VMEM((1, LATS), F32),
            pltpu.VMEM((1, FEAT), F32),
            pltpu.VMEM((4, 64, LATS), jnp.int32),
            pltpu.VMEM((2, TOK, LATS), BF16),
            pltpu.VMEM((CH, LATS), F32),
            pltpu.VMEM((2, 4, 64, LATS), F32),
            pltpu.VMEM((2, 4, 3, 64, LATS), BF16),
            pltpu.VMEM((2, 4, 64, LATS), BF16),
            pltpu.VMEM((2, 4, 64, LATS), BF16),
            pltpu.VMEM((TOK, LATS), BF16),
            pltpu.VMEM((TOK, LATS), BF16),
            pltpu.VMEM((TOK, FEAT), F32),
            pltpu.VMEM((4, 128, FEAT), F32),
            pltpu.VMEM((2, len(SUM), H, FEAT), BF16),
            pltpu.VMEM((2, len(SUM), H, FEAT), BF16),
            pltpu.VMEM((FEAT, LATS), BF16),
            pltpu.VMEM((LATS, FEAT), BF16),
            pltpu.VMEM((B, FEAT), BF16),
            dma((8, 4)), dma((7,)),
            dma((2, 2, max(map(len, SPREAD)))), dma((2, 2, max(map(len, SPREAD)))), dma((2, 2, 4)), dma((2, 2, 4)),
            dma((2, 4, 3)), dma((2, 4, 3)), dma((2, 4)), dma((2, 4)), dma((2, 4, 3)), dma((2, 4, 3)),
            dma((4, 2)), dma((4, 2)), dma((2, len(SUM))), dma((2, len(SUM))),
        ],
        compiler_params=pltpu.CompilerParams(
            collective_id=0, has_side_effects=True, vmem_limit_bytes=58 << 20
        ),
        cost_estimate=pl.CostEstimate(flops=10 * 1024 * 2048 * 512, bytes_accessed=14 << 20, transcendentals=0),
    )(
        stacked, enc_weight, enc_bias.reshape(1, -1), dec_weight, dec_bias.reshape(1, -1), active, upstream
    )
    return pl.pallas_call(
        copy_out,
        out_shape=shapes,
        in_specs=[hbm] * 3,
        out_specs=(hbm,) * 3,
        scratch_shapes=[
            pltpu.VMEM((B, FEAT), BF16),
            pltpu.VMEM((FEAT, LATS), BF16),
            pltpu.VMEM((LATS, FEAT), BF16),
            dma((2, 9)),
        ],
        compiler_params=pltpu.CompilerParams(vmem_limit_bytes=58 << 20),
        cost_estimate=pl.CostEstimate(flops=0, bytes_accessed=9 << 20, transcendentals=0),
    )(*outs)


def solution(mesh):
    placed = (
        P("lat", "section"),
        P("section", "lat"),
        P("lat"),
        P("lat", "section"),
        P("section"),
        P(None, "lat"),
        P("lat", "section"),
    )
    return jax.shard_map(
        per_device,
        mesh=mesh,
        in_specs=placed,
        out_specs=(P("lat", "section"), P("section", "lat"), P("lat", "section")),
        check_vma=False,
    )
```

time: 550 us -> 89.6 us (0.16)
  waiting for transfers between devices: 496 us -> 0 us
  Pallas kernels: 0 us -> 87.8 us
  matrix products: 31.3 us -> 0 us
  between operations: 13.8 us -> 0.64 us
    psum x1 -> x0, waiting for transfers between devices: 184 us -> none  [per_device(): preact = lax.psum(partial_value, 'section') + enc_bias]
    all_gather x2 -> x0, waiting for transfers between devices: 172 us -> none  [the longest x1 91.8 us: per_device(): upstream_all = lax.all_gather(upstream, 'lat', axis=0, tiled=True)]
    reduce_scatter x1 -> x0, waiting for transfers between devices: 138 us -> none  [per_device(): lax.psum_scatter(jnp.dot(latent, dec_weight, preferred_element_type=jnp.f...]
    pallas_call x0 -> x2, Pallas kernels: none -> 87.8 us  [the longest x1 84 us: per_device(): pl.pallas_call(kernel, out_shape=shapes, in_specs=[hbm] * 7, out_specs=(h...]
    dot_general x5 -> x0, matrix products: 31.3 us -> none  [the longest x1 7.34 us: per_device(): lax.dot_general(stacked_all, pre_grad, (((0,), (0,)), ((), ())), preferre...]
  transfers between devices with their start and end apart: 4 -> 0, of which waited for: 4 -> 0; matrix products, arithmetic and copies ran while one was open for 4% -> 0% of each run, Pallas kernels for 0% -> 0%
where the time goes in v2:
time: 89.6 us; the launch traced here: 88.4 us
  Pallas kernels  87.8 us (98%)
    pallas_call x1, Pallas kernels, per_device(): pl.pallas_call(kernel, out_shape=shapes, in_specs=[hbm] * 7, out_specs=(h...  84 us
    pallas_call x1, Pallas kernels, per_device(): pl.pallas_call(copy_out, out_shape=shapes, in_specs=[hbm] * 3, out_specs=...  3.81 us

profile of v2, /device:TPU:8, one launch (start us, length us, event | category | flops | bytes accessed | tf_op | source)
XLA Modules:
  0.0 88.4 jit_solution(4664737998093567139)
XLA Ops:
  0.6 84.0 %shard_map.94 = (bf16[32,2048]{1,0:T(8,128)(2,1)}, bf16[2048,512]{1,0:T(8,128)(2,1)}, bf16[512,2048]{1,0:T(8,128)(2,1)}) custom-call(bf16[32,2048]{1,0:T(8,128)(2,1)} %x_hbm.1, bf16[2048,512]{1,0:T(8,128)(2,1)} %we_hbm.1, f32[1,512]{1,0:T(1,128)} %bitcast.3, bf16[512,2048]{1,0:T(8,128)(2,1)} %wd_hbm.1, f32[1,2048]{1,0:T(1,128)} %bitcast.2, ...), custom_call_target="tpu_custom_call" | custom-call | flops 10737418240 | bytes 14680064 | tf_op jit(solution)/shard_map/pallas_call | solution.py:381
  84.6 3.8 %shard_map.95 = (bf16[32,2048]{1,0:T(8,128)(2,1)}, bf16[2048,512]{1,0:T(8,128)(2,1)}, bf16[512,2048]{1,0:T(8,128)(2,1)}) custom-call(bf16[32,2048]{1,0:T(8,128)(2,1)} %get-tuple-element.6.reb, bf16[2048,512]{1,0:T(8,128)(2,1)} %get-tuple-element.7.ge, bf16[512,2048]{1,0:T(8,128)(2,1)} %get-tuple-element.8.gd), custom_call_target="tpu_custom_call" | custom-call | bytes 9437184 | tf_op jit(solution)/shard_map/pallas_call | solution.py:421

commit v3 on v2

--- a/solution.py
+++ b/solution.py
@@ -41,10 +41,10 @@
 )
 SPREAD = (SPREAD_X, SPREAD_UP)
 SUM = (
-    (1, "z", 2, (4, 1), (2, 1)), (0, "z", -2, (4, 1), (6, 1)), (None, "z", -1, (5, 1), (6, 1)),
+    (1, "z", 1, (4, 1), (3, 1)), (0, "z", -1, (4, 1), (5, 1)), (None, "z", -1, (5, 1), (6, 1)),
     (None, "z", 1, (3, 1), (2, 1)), (None, "x", 0, (7, 1), (7, 0)), (None, "x", 0, (1, 1), (1, 0)),
-    (None, "z", -1, (5, 0), (6, 0)), (None, "z", 1, (3, 0), (2, 0)), (None, "x", 0, (6, 1), (6, 0)),
-    (None, "x", 0, (2, 1), (2, 0)), (1, "z", -2, (4, 0), (6, 0)), (0, "z", 2, (4, 0), (2, 0)),
+    (1, "z", -1, (4, 0), (5, 0)), (0, "z", 1, (4, 0), (3, 0)), (None, "z", -1, (5, 0), (6, 0)),
+    (None, "z", 1, (3, 0), (2, 0)), (None, "x", 0, (6, 1), (6, 0)), (None, "x", 0, (2, 1), (2, 0)),
     (None, "x", 0, (0, 1), (0, 0)), (None, "z", -1, (7, 0), (0, 0)), (None, "z", 1, (1, 0), (0, 0)),
     (None, "z", -2, (6, 0), (0, 0)), (None, "z", 2, (2, 0), (0, 0)),
 )
@@ -64,34 +64,34 @@
     ("take", 0, 1, 2, 0), ("take", 0, 1, 6, 0), ("take", 0, 0, 7, 1), ("share", 0, 0, 0),
     ("take", 0, 1, 1, 1), ("take", 0, 0, 3, 0), ("take", 0, 0, 5, 0), ("take", 0, 1, 7, 1),
     ("share", 0, 1, 0), ("take", 0, 1, 3, 0), ("take", 0, 1, 5, 0), ("take", 0, 0, 2, 1),
-    ("take", 0, 0, 4, 0), ("take", 0, 0, 6, 1), ("share", 0, 0, 1), ("take", 0, 1, 4, 0),
-    ("take", 0, 1, 2, 1), ("take", 1, 0, 0, 0), ("sec_a", 0, 0), ("take", 0, 0, 3, 1), ("take", 0, 1, 6, 1),
+    ("take", 0, 0, 6, 1), ("take", 0, 0, 4, 0), ("share", 0, 0, 1), ("take", 1, 0, 0, 0),
+    ("take", 0, 1, 2, 1), ("take", 0, 1, 4, 0), ("sec_a", 0, 0), ("take", 0, 0, 3, 1), ("take", 0, 1, 6, 1),
     ("share", 0, 1, 1), ("take", 1, 1, 0, 0), ("take", 0, 0, 5, 1), ("share", 0, 0, 2), ("take", 0, 0, 4, 1),
-    ("share", 0, 0, 3), ("sec_a", 0, 2), ("take", 0, 1, 3, 1), ("take", 0, 1, 4, 1), ("share", 0, 1, 3),
-    ("take", 1, 0, 7, 0), ("sec_a", 0, 1), ("take", 0, 1, 5, 1), ("share", 0, 1, 2), ("take", 1, 0, 0, 1),
-    ("take", 1, 0, 1, 0), ("take", 1, 1, 1, 0), ("sec_b", 0, 0), ("take", 1, 1, 0, 1), ("take", 1, 1, 7, 0),
-    ("sec_a", 0, 3), ("take", 1, 0, 6, 0), ("take", 1, 0, 7, 1), ("sec_b", 0, 2), ("take", 1, 0, 2, 0),
-    ("take", 1, 0, 1, 1), ("share", 1, 0, 0), ("take", 1, 1, 6, 0), ("take", 1, 1, 2, 0),
-    ("take", 1, 1, 1, 1), ("sec_b", 0, 1), ("take", 1, 0, 5, 0), ("sec_c", 0, 0), ("take", 1, 0, 3, 0),
-    ("take", 1, 0, 6, 1), ("take", 1, 1, 7, 1), ("share", 1, 1, 0), ("sec_c", 0, 2), ("sec_b", 0, 3),
-    ("take", 1, 0, 2, 1), ("take", 1, 1, 5, 0), ("share", 1, 0, 1), ("sec_c", 0, 1), ("take", 1, 1, 3, 0),
-    ("take", 1, 0, 5, 1), ("sec_a", 1, 0), ("decode", 0), ("sec_c", 0, 3), ("take", 1, 0, 4, 0),
-    ("take", 1, 1, 2, 1), ("take", 1, 1, 6, 1), ("take", 1, 1, 4, 0), ("share", 1, 1, 1),
-    ("take", 1, 0, 3, 1), ("share", 1, 0, 2), ("decode", 2), ("collect", 0, 0), ("reduce", 0, 1, 1),
-    ("reduce", 0, 7, 1), ("take", 1, 0, 4, 1), ("share", 1, 0, 3), ("collect", 0, 1), ("decode", 1),
-    ("take", 1, 1, 3, 1), ("take", 1, 1, 5, 1), ("sec_a", 1, 2), ("collect", 2, 0), ("reduce", 1, 1, 1),
-    ("reduce", 1, 7, 1), ("share", 1, 1, 2), ("reduce", 0, 1, 0), ("sec_b", 1, 0), ("collect", 2, 1),
-    ("sec_a", 1, 1), ("reduce", 0, 7, 0), ("take", 1, 1, 4, 1), ("share", 1, 1, 3), ("collect", 1, 0),
-    ("reduce", 0, 3, 1), ("reduce", 0, 5, 1), ("reduce", 0, 3, 0), ("reduce", 0, 5, 0), ("decode", 3),
-    ("reduce", 1, 1, 0), ("collect", 1, 1), ("reduce", 0, 4, 1), ("reduce", 0, 4, 0), ("reduce", 0, 0, 1),
-    ("sec_a", 1, 3), ("reduce", 1, 7, 0), ("reduce", 0, 2, 1), ("sec_c", 1, 0), ("collect", 3, 0),
-    ("reduce", 1, 3, 1), ("reduce", 1, 5, 1), ("reduce", 1, 3, 0), ("reduce", 1, 5, 0), ("sec_b", 1, 2),
-    ("collect", 3, 1), ("reduce", 1, 4, 1), ("reduce", 1, 4, 0), ("reduce", 1, 0, 1), ("sec_b", 1, 1),
-    ("dec_grad", 0), ("dec_grad", 1), ("reduce", 0, 6, 1), ("reduce", 0, 2, 0), ("sec_b", 1, 3),
-    ("sec_c", 1, 2), ("dec_grad", 2), ("dec_grad", 3), ("sec_c", 1, 1), ("reduce", 1, 6, 1), ("sec_e", 1, 0),
-    ("reduce", 0, 6, 0), ("sec_c", 1, 3), ("reduce", 1, 2, 1), ("sec_e", 1, 2), ("reduce", 1, 6, 0),
-    ("sec_e", 1, 1), ("finish", 0), ("reduce", 1, 2, 0), ("sec_e", 1, 3), ("enc_grad", 0), ("enc_grad", 1),
-    ("enc_grad", 2), ("finish", 1), ("enc_grad", 3),
+    ("share", 0, 0, 3), ("sec_a", 0, 2), ("take", 1, 0, 1, 0), ("take", 1, 0, 7, 0), ("take", 1, 0, 0, 1),
+    ("sec_a", 0, 1), ("take", 0, 1, 3, 1), ("take", 0, 1, 5, 1), ("share", 0, 1, 2), ("take", 0, 1, 4, 1),
+    ("share", 0, 1, 3), ("sec_b", 0, 0), ("take", 1, 1, 1, 0), ("take", 1, 1, 7, 0), ("take", 1, 1, 0, 1),
+    ("take", 1, 0, 2, 0), ("sec_a", 0, 3), ("take", 1, 0, 1, 1), ("take", 1, 0, 6, 0), ("sec_b", 0, 2),
+    ("take", 1, 0, 7, 1), ("share", 1, 0, 0), ("take", 1, 1, 2, 0), ("sec_c", 0, 0), ("take", 1, 1, 6, 0),
+    ("sec_b", 0, 1), ("take", 1, 0, 3, 0), ("take", 1, 1, 1, 1), ("take", 1, 0, 5, 0), ("take", 1, 0, 2, 1),
+    ("take", 1, 1, 7, 1), ("share", 1, 1, 0), ("sec_c", 0, 2), ("take", 1, 0, 6, 1), ("sec_b", 0, 3),
+    ("take", 1, 1, 3, 0), ("share", 1, 0, 1), ("take", 1, 1, 5, 0), ("sec_c", 0, 1), ("take", 1, 0, 4, 0),
+    ("sec_a", 1, 0), ("decode", 0), ("take", 1, 0, 5, 1), ("sec_c", 0, 3), ("take", 1, 0, 3, 1),
+    ("take", 1, 1, 2, 1), ("take", 1, 1, 6, 1), ("share", 1, 0, 2), ("share", 1, 1, 1), ("take", 1, 1, 4, 0),
+    ("decode", 2), ("collect", 0, 0), ("collect", 0, 1), ("reduce", 0, 1, 1), ("reduce", 0, 7, 1),
+    ("sec_a", 1, 2), ("decode", 1), ("collect", 2, 0), ("collect", 2, 1), ("take", 1, 0, 4, 1),
+    ("reduce", 1, 1, 1), ("reduce", 1, 7, 1), ("take", 1, 1, 3, 1), ("take", 1, 1, 5, 1), ("share", 1, 0, 3),
+    ("share", 1, 1, 2), ("collect", 1, 0), ("reduce", 0, 3, 1), ("sec_b", 1, 0), ("collect", 1, 1),
+    ("reduce", 0, 4, 1), ("reduce", 0, 4, 0), ("reduce", 0, 5, 0), ("sec_a", 1, 1), ("reduce", 0, 0, 1),
+    ("reduce", 0, 1, 0), ("reduce", 0, 7, 0), ("take", 1, 1, 4, 1), ("share", 1, 1, 3), ("decode", 3),
+    ("reduce", 0, 2, 1), ("reduce", 1, 1, 0), ("reduce", 1, 7, 0), ("sec_a", 1, 3), ("sec_c", 1, 0),
+    ("collect", 3, 0), ("sec_b", 1, 2), ("collect", 3, 1), ("reduce", 1, 4, 1), ("reduce", 0, 5, 1),
+    ("reduce", 1, 4, 0), ("reduce", 1, 5, 1), ("reduce", 0, 3, 0), ("reduce", 1, 3, 0), ("reduce", 1, 0, 1),
+    ("dec_grad", 0), ("sec_b", 1, 1), ("dec_grad", 1), ("dec_grad", 2), ("sec_c", 1, 2), ("reduce", 1, 3, 1),
+    ("sec_b", 1, 3), ("reduce", 0, 6, 1), ("reduce", 1, 5, 0), ("reduce", 0, 2, 0), ("dec_grad", 3),
+    ("sec_c", 1, 1), ("reduce", 1, 6, 1), ("sec_e", 1, 0), ("reduce", 1, 2, 1), ("sec_c", 1, 3),
+    ("reduce", 0, 6, 0), ("sec_e", 1, 2), ("enc_near", 0), ("enc_near", 1), ("reduce", 1, 6, 0),
+    ("enc_near", 2), ("enc_near", 3), ("reduce", 1, 2, 0), ("sec_e", 1, 1), ("finish", 0), ("sec_e", 1, 3),
+    ("enc_grad", 0), ("enc_grad", 1), ("enc_grad", 2), ("finish", 1), ("enc_grad", 3),
 )
 
 def kernel(
@@ -99,7 +99,7 @@
     reb_hbm, ge_hbm, gd_hbm,
     xs, us, we, wd, be, bd, act,
     part, full, own, yin, xout, xin, lat, pre,
-    dec, cin, stage, sums_in, ge, gd, reb,
+    dec, cout, cin, stage, sums_in, part_ge, ge, gd, reb,
     load_sem, store_sem, g_s, g_r, gc_s, gc_r,
     ry_s, ry_r, rx_s, rx_r, ay_s, ay_r, dc_s, dc_r, s_s, s_r,
 ):
@@ -255,8 +255,8 @@
             ay(t, q, k).wait_recv()
 
     def dc(q, p):
-        rows = pl.ds(q * CH + 128 + p * 64, 64)
-        return remote(dec.at[rows], cin.at[q, pl.ds(p * 64, 64)], (dc_s, dc_r), (q, p), cdev)
+        rows = pl.ds(p * 64, 64)
+        return remote(cout.at[q, rows], cin.at[q, rows], (dc_s, dc_r), (q, p), cdev)
 
     def decode(q):
         sec_e(0, q)
@@ -264,9 +264,9 @@
         @pl.loop(0, 4)
         def _(n):
             cols = pl.ds(pl.multiple_of(n * 512, 512), 512)
-            dec[pl.ds(q * CH, CH), cols] = jnp.dot(
-                lat[pl.ds(q * CH, CH)], wd[:, cols], preferred_element_type=F32
-            )
+            both = jnp.dot(lat[pl.ds(q * CH, CH)], wd[:, cols], preferred_element_type=F32)
+            dec[q, :, cols] = both[:128]
+            cout[q, :, cols] = both[128:].astype(BF16)
 
         start(dc(q, 0))
         start(dc(q, 1))
@@ -279,7 +279,8 @@
 
     def total(a, d, half, cols):
         group, place = divmod(PLACE[d], 4)
-        value = dec[pl.ds(row(a, d, 0, half), H), cols] + cin[2 * a + group, pl.ds(place * 32 + half * H, H), cols]
+        rows = pl.ds(place * 32 + half * H, H)
+        value = dec[2 * a + group, rows, cols] + cin[2 * a + group, rows, cols].astype(F32)
         for i in coming(SUM, a, (d, half)):
             value = value + sums_in[a, i, :, cols].astype(F32)
         return value
@@ -321,12 +322,24 @@
         if n == 3:
             store(pltpu.make_async_copy(gd, gd_hbm, store_sem.at[2]))
 
+    def enc_tokens(rows, group):
+        value = 0.0
+        for q in (group, 2 + group):
+            at = pl.ds(q * CH, CH)
+            value = value + lax.dot_general(
+                xs[at, rows], pre[at], (((0,), (0,)), ((), ())), preferred_element_type=F32
+            )
+        return value
+
+    def enc_near(n):
+        for m in (0, 1):
+            rows = pl.ds(n * 512 + m * 256, 256)
+            part_ge[rows] = enc_tokens(rows, 0)
+
     def enc_grad(n):
         for m in (0, 1):
             rows = pl.ds(n * 512 + m * 256, 256)
-            ge[rows] = lax.dot_general(
-                xs[:, rows], pre[...], (((0,), (0,)), ((), ())), preferred_element_type=F32
-            ).astype(BF16)
+            ge[rows] = (part_ge[rows] + enc_tokens(rows, 1)).astype(BF16)
         rows = pl.ds(n * 512, 512)
         store(pltpu.make_async_copy(ge.at[rows], ge_hbm.at[rows], store_sem.at[3 + n]))
 
@@ -337,7 +350,8 @@
     phases = {
         f.__name__: f
         for f in (
-            ready, take, share, sec_a, sec_b, sec_c, sec_e, decode, collect, reduce, finish, dec_grad, enc_grad
+            ready, take, share, sec_a, sec_b, sec_c, sec_e, decode, collect, reduce, finish, dec_grad, enc_near,
+            enc_grad,
         )
     }
     plan = [(phases[name], args) for name, *args in PLAN]
@@ -399,10 +413,12 @@
             pltpu.VMEM((2, 4, 64, LATS), BF16),
             pltpu.VMEM((TOK, LATS), BF16),
             pltpu.VMEM((TOK, LATS), BF16),
-            pltpu.VMEM((TOK, FEAT), F32),
             pltpu.VMEM((4, 128, FEAT), F32),
+            pltpu.VMEM((4, 128, FEAT), BF16),
+            pltpu.VMEM((4, 128, FEAT), BF16),
             pltpu.VMEM((2, len(SUM), H, FEAT), BF16),
             pltpu.VMEM((2, len(SUM), H, FEAT), BF16),
+            pltpu.VMEM((FEAT, LATS), F32),
             pltpu.VMEM((FEAT, LATS), BF16),
             pltpu.VMEM((LATS, FEAT), BF16),
             pltpu.VMEM((B, FEAT), BF16),

time: 89.6 us -> 85.6 us (0.955)
  Pallas kernels: 87.8 us -> 83.8 us
    pallas_call x1, Pallas kernels: 84 us -> 80 us  [per_device(): pl.pallas_call(kernel, out_shape=shapes, in_specs=[hbm] * 7, out_specs=(h...]
where the time goes in v3:
time: 85.6 us; the launch traced here: 84.4 us
  Pallas kernels  83.8 us (98%)
    pallas_call x1, Pallas kernels, per_device(): pl.pallas_call(kernel, out_shape=shapes, in_specs=[hbm] * 7, out_specs=(h...  80 us
    pallas_call x1, Pallas kernels, per_device(): pl.pallas_call(copy_out, out_shape=shapes, in_specs=[hbm] * 3, out_specs=...  3.81 us

profile of v3, /device:TPU:8, one launch (start us, length us, event | category | flops | bytes accessed | tf_op | source)
XLA Modules:
  0.0 84.4 jit_solution(9356960566699795335)
XLA Ops:
  0.6 80.0 %shard_map.94 = (bf16[32,2048]{1,0:T(8,128)(2,1)}, bf16[2048,512]{1,0:T(8,128)(2,1)}, bf16[512,2048]{1,0:T(8,128)(2,1)}) custom-call(bf16[32,2048]{1,0:T(8,128)(2,1)} %x_hbm.1, bf16[2048,512]{1,0:T(8,128)(2,1)} %we_hbm.1, f32[1,512]{1,0:T(1,128)} %bitcast.3, bf16[512,2048]{1,0:T(8,128)(2,1)} %wd_hbm.1, f32[1,2048]{1,0:T(1,128)} %bitcast.2, ...), custom_call_target="tpu_custom_call" | custom-call | flops 10737418240 | bytes 14680064 | tf_op jit(solution)/shard_map/pallas_call | solution.py:395
  80.6 3.8 %shard_map.95 = (bf16[32,2048]{1,0:T(8,128)(2,1)}, bf16[2048,512]{1,0:T(8,128)(2,1)}, bf16[512,2048]{1,0:T(8,128)(2,1)}) custom-call(bf16[32,2048]{1,0:T(8,128)(2,1)} %get-tuple-element.6.reb, bf16[2048,512]{1,0:T(8,128)(2,1)} %get-tuple-element.7.ge, bf16[512,2048]{1,0:T(8,128)(2,1)} %get-tuple-element.8.gd), custom_call_target="tpu_custom_call" | custom-call | bytes 9437184 | tf_op jit(solution)/shard_map/pallas_call | solution.py:437
